TPU v7x, 32 devices: a whole 2x2x4 slice. The times are simulated.
32 devices in a mesh: region: 2 (over y), snp: 8 (over z, x), sample: 2 (over core).
Axes of the slice: x: 2, y: 2, z: 4, core: 2. Of those that a mesh axis runs over, the one named last changes fastest.
Arguments:
- dosage: bfloat16 [4096, 24576], P('sample', ('region', 'snp')), parts along dimension 1, as said below
- partners: int32 [48, 3], P(('region', 'snp')), parts along dimension 0, may hold values from -1 to 23, as said below
Outputs:
- ld_tiles: float32 [48, 3, 512, 512], P(('region', 'snp'), None, 'sample'), parts along dimension 0
There are 2 independent parts, one for each index of `region`. A program takes and returns all parts, laid end to end along the dimension named above; each array names one. Nothing has to cross between parts.
Inputs may be any that keep to these rules, and one draw needn't show every extreme that they name: For each block b: partners[b, 0] = b; the other entries are distinct blocks b + 1 to b + 2 in rising order, followed by -1 entries only; block 0 lists all 3 blocks 0 to 2. `dosage`: dosages are real values within 0 and 2.
All inputs are finite; a program needn't handle non-finite values.
Results may differ from a plain program's by a relative error of at most 0.0013.
Values may be sent and summed in bfloat16 or wider, within the bound.
A program may use at most 128 MiB of HBM per device.

v0:
```python
import jax
import jax.numpy as jnp
from jax import lax
from jax.sharding import PartitionSpec as P

BLOCK = 512
REACH = 2


def shifted(block, axis, distance):
    devices = range(lax.axis_size(axis))
    route = [(i - distance, i) for i in devices if i - distance in devices]
    return lax.ppermute(block, axis, route)


def panel_product(own, panel):
    return lax.dot_general(own, panel, (((0,), (0,)), ((), ())), preferred_element_type=jnp.float32)


def on_device(dosage, partners):
    samples_total = dosage.shape[0] * lax.axis_size("sample")
    width = BLOCK
    values = dosage.astype(jnp.float32)
    total, square_total = lax.psum(
        (jnp.sum(values, axis=0), jnp.sum(values * values, axis=0)), "sample"
    )
    mean = total / samples_total
    variance = square_total / samples_total - mean * mean
    scale = lax.rsqrt(variance + 1e-05)
    standard = ((values - mean[None, :]) * scale[None, :]).astype(jnp.bfloat16)
    upper = shifted(standard, "snp", -1)[:, : REACH * width]
    extended = jnp.concatenate([standard, upper], axis=1)
    blocks_here = partners.shape[0]
    results = []
    for local in range(blocks_here):
        own = standard[:, local * width : (local + 1) * width]
        listed = partners[local]
        offsets = listed - listed[0]
        valid = listed >= 0
        panel = extended[:, local * width : (local + REACH + 1) * width]
        every = panel_product(own, panel).reshape(width, REACH + 1, width).transpose(1, 0, 2)
        choose = (offsets[:, None] == jnp.arange(REACH + 1, dtype=jnp.int32)[None, :]) & valid[
            :, None
        ]
        picked = jnp.where(choose[:, :, None, None], every[None, :, :, :], 0.0)
        results.append(jnp.sum(picked, axis=1))
    partial_value = jnp.stack(results)
    summed = lax.psum_scatter(partial_value, "sample", scatter_dimension=2, tiled=True)
    return summed / samples_total


def solution(mesh):
    in_specs = (P("sample", ("region", "snp")), P(("region", "snp"), None))
    out_specs = P(("region", "snp"), None, "sample", None)
    return jax.shard_map(
        on_device, mesh=mesh, in_specs=in_specs, out_specs=out_specs, check_vma=False
    )
```

profile of v0, /device:TPU:0, one launch (start us, length us, event | category | flops | bytes accessed | tf_op | source)
XLA Modules:
  0.0 228.2 jit_solution(17649018244329381241)
XLA Ops:
  6.5 0.0 reduce-scatter.2.cloned.1.call-start
  6.5 4.5 %convert_reduce_fusion = (f32[1536]{0:T(1024)S(1)}, f32[1536]{0:T(1024)S(1)}) fusion(bf16[2048,1536]{1,0:T(8,128)(2,1)} %param.2), kind=kLoop, calls=%fused_computation.2 | loop fusion | flops 12579840 | bytes 6303744 | tf_op jit(solution)/shard_map/reduce_sum | solution.py:25
  11.0 3.6 %all-reduce = (f32[1536]{0:T(1024)S(1)}, f32[1536]{0:T(1024)S(1)}) all-reduce(f32[1536]{0:T(1024)S(1)} %get-tuple-element.6, f32[1536]{0:T(1024)S(1)} %get-tuple-element.5), channel_id=1, replica_groups=mesh['region'=2,'snp'=8,'sample'=2] {'sample'}, use_global_device_ids=true, to_apply=%region_3.0 | all-reduce | flops 3072 | bytes 24576 | tf_op jit(solution)/shard_map/psum | solution.py:24
  14.6 7.0 %fusion.1 = bf16[2048,1536]{1,0:T(8,128)(2,1)} fusion(bf16[2048,1536]{1,0:T(8,128)(2,1)} %param.2, f32[1536]{0:T(1024)S(1)} %get-tuple-element.10, f32[1536]{0:T(1024)S(1)} %get-tuple-element.9), kind=kLoop, calls=%fused_computation.4 | loop fusion | flops 12582912 | bytes 12595200 | tf_op jit(solution)/shard_map/convert_element_type | solution.py:30
  21.6 1.5 collective-permute-start
  23.1 6.3 %fusion.10 = f32[512,1536]{0,1:T(8,128)S(1)} fusion(bf16[2048,1536]{1,0:T(8,128)(2,1)} %fusion.1), kind=kOutput, calls=%fused_computation.20 | convolution fusion | flops 3221225472 | bytes 11534336 | tf_op jit(solution)/shard_map/dot_general | solution.py:17
  29.3 0.0 copy-start.1
  29.3 2.4 %copy.13 = f32[3,512,512]{2,1,0:T(8,128)} copy(f32[3,512,512]{1,2,0:T(8,128)S(1)} %bitcast.33) | data formatting | bytes 6291456 | tf_op jit(solution)/shard_map/transpose | solution.py:41
  31.7 0.0 copy-done.1
  31.7 0.6 fusion.17
  32.3 1.9 subtract_bitcast_fusion.2
  34.2 0.1 fusion.14
  34.3 0.1 fusion.12
  34.4 3.0 %select_reduce_fusion.2 = f32[3,512,512]{2,1,0:T(8,128)S(1)} fusion(f32[3,512,512]{2,1,0:T(8,128)} %copy.13, pred[3,3]{1,0:T(4,128)(4,1)S(1)} %get-tuple-element.20), kind=kLoop, calls=%fused_computation.11 | loop fusion | flops 3932160 | bytes 6291465 | tf_op jit(solution)/shard_map/reduce_sum | solution.py:46
  37.4 125.1 %collective-permute-done = bf16[2048,1536]{1,0:T(8,128)(2,1)} collective-permute-done((bf16[2048,1536]{1,0:T(8,128)(2,1)}, bf16[2048,1536]{1,0:T(8,128)(2,1)}, u32[]{:S(2)}, u32[]{:S(2)}) %collective-permute-start) | collective-permute-done | bytes 6291488 | tf_op jit(solution)/shard_map/ppermute | solution.py:13
  162.5 2.6 %slice.56 = bf16[2048,1024]{1,0:T(8,128)(2,1)S(1)} slice(bf16[2048,1536]{1,0:T(8,128)(2,1)} %collective-permute-done), slice={[0:2048], [0:1024]} | slice | bytes 8388608 | tf_op jit(solution)/shard_map/slice | solution.py:31
  165.1 8.0 %fusion.4 = f32[512,1536]{0,1:T(8,128)} fusion(bf16[2048,1536]{1,0:T(8,128)(2,1)} %fusion.1, bf16[2048,1024]{1,0:T(8,128)(2,1)S(1)} %slice.56), kind=kOutput, calls=%fused_computation.13 | convolution fusion | flops 3233808384 | bytes 15728640 | tf_op jit(solution)/shard_map/dot_general | solution.py:17
  173.1 7.4 %fusion.6 = f32[512,1536]{0,1:T(8,128)} fusion(bf16[2048,1024]{1,0:T(8,128)(2,1)S(1)} %slice.56, bf16[2048,1536]{1,0:T(8,128)(2,1)} %fusion.1), kind=kOutput, calls=%fused_computation.15 | convolution fusion | flops 3233808384 | bytes 15728640 | tf_op jit(solution)/shard_map/dot_general | solution.py:17
  180.5 3.6 %copy.15 = f32[3,512,512]{2,1,0:T(8,128)} copy(f32[3,512,512]{1,2,0:T(8,128)} %bitcast.32) | data formatting | bytes 6291456 | tf_op jit(solution)/shard_map/transpose | solution.py:41
  184.0 3.6 %copy.17 = f32[3,512,512]{2,1,0:T(8,128)} copy(f32[3,512,512]{1,2,0:T(8,128)} %bitcast.31) | data formatting | bytes 6291456 | tf_op jit(solution)/shard_map/transpose | solution.py:41
  187.6 0.0 copy-start
  187.6 3.3 %select_reduce_fusion.1 = f32[3,512,512]{2,1,0:T(8,128)S(1)} fusion(f32[3,512,512]{2,1,0:T(8,128)} %copy.15, pred[3,3]{1,0:T(4,128)(4,1)S(1)} %get-tuple-element.21), kind=kLoop, calls=%fused_computation.10 | loop fusion | flops 3932160 | bytes 6291465 | tf_op jit(solution)/shard_map/reduce_sum | solution.py:46
  190.9 0.0 copy-done
  190.9 0.8 select_reduce_fusion
  191.7 5.0 %pad_maximum_fusion = f32[3,3,512,512]{3,2,1,0:T(8,128)} fusion(f32[1,3,512,512]{3,2,1,0:T(8,128)S(1)} %bitcast.30, f32[1,3,512,512]{3,2,1,0:T(8,128)S(1)} %bitcast.29, f32[1,3,512,512]{3,2,1,0:T(8,128)S(1)} %bitcast.28), kind=kLoop, calls=%fused_computation.8 | loop fusion | flops 4718592 | bytes 18874368 | tf_op jit(solution)/shard_map/stack | solution.py:47
  196.7 0.0 reduce-scatter.2.cloned.1.call-update
  196.7 19.3 %reduce-scatter.2.cloned.1.call-done = f32[3,3,256,512]{3,2,1,0:T(8,128)} async-done(((f32[3,3,512,512]{3,2,1,0:T(8,128)}), f32[3,3,256,512]{3,2,1,0:T(8,128)}) %reduce-scatter.2.cloned.1.call-update) | async-done | bytes 4718608 | tf_op jit(solution)/shard_map/reduce_scatter | solution.py:48
  216.1 5.3 %broadcast_multiply_fusion = f32[3,3,256,512]{3,2,1,0:T(8,128)} fusion(f32[3,3,256,512]{3,2,1,0:T(8,128)} %reduce-scatter.2.cloned.1.call-done), kind=kLoop, calls=%fused_computation.17 | loop fusion | flops 1179648 | bytes 9437184 | tf_op jit(solution)/shard_map/div | solution.py:49
  (2 shorter events, 0.0 us)
Async XLA Ops:
  6.5 209.5 %reduce-scatter.2.cloned.1.call-start = ((), (), s32[]{:S(2)}) async-start(), calls=%async_computation.1 | async-start | bytes 14155776 | tf_op jit(solution)/shard_map/reduce_scatter | solution.py:48
  21.6 140.9 %collective-permute-start = (bf16[2048,1536]{1,0:T(8,128)(2,1)}, bf16[2048,1536]{1,0:T(8,128)(2,1)}, u32[]{:S(2)}, u32[]{:S(2)}) collective-permute-start(bf16[2048,1536]{1,0:T(8,128)(2,1)} %fusion.1), channel_id=1, source_target_pairs={{2,0},{4,2},{6,4},{8,6},{10,8},{12,10},{14,12},{3,1},{5,3},{7,5},{... | collective-permute-start | bytes 18874376 | tf_op jit(solution)/shard_map/ppermute | solution.py:13
  29.3 2.4 %copy-start.1 = (s32[3,3]{1,0:T(4,128)S(1)}, s32[3,3]{1,0:T(4,128)}, u32[]{:S(2)}) copy-start(s32[3,3]{1,0:T(4,128)} %param.3) | copy-start | bytes 112
  187.6 3.3 %copy-start = (f32[3,512,512]{2,1,0:T(8,128)S(1)}, f32[3,512,512]{2,1,0:T(8,128)}, u32[]{:S(2)}) copy-start(f32[3,512,512]{2,1,0:T(8,128)} %copy.17) | copy-start | bytes 9437188
Sparse Core Ops, SparseCore 0:
  196.9 19.1 reduce-scatter.1
where the time goes:
time: 229 us; the launch traced here: 228 us
  waiting for transfers between devices  144 us (63%)
  other arithmetic  30.9 us (13%)
  matrix products  21.6 us (9%)
  between operations  13.5 us (6%)
  local copies, waits for them, and re-layouts  12.7 us (6%)
  blocking collectives  3.57 us (2%)
    ppermute x1, waiting for transfers between devices, shifted(): return lax.ppermute(block, axis, route)  125 us
    dot_general x3, matrix products, panel_product(): lax.dot_general(own, panel, (((0,), (0,)), ((), ())), preferred_element_t...  21.6 us
    reduce_scatter x1, waiting for transfers between devices, on_device(): lax.psum_scatter(partial_value, 'sample', scatter_dimension=2, tiled=True)  19.3 us
    transpose x3, local copies, waits for them, and re-layouts, on_device(): panel_product(own, panel).reshape(width, REACH + 1, width)  9.52 us
    reduce_sum x3, other arithmetic, on_device(): results.append(jnp.sum(picked, axis=1))  7.11 us
    convert_element_type x1, other arithmetic, on_device(): standard = ((values - mean[None, :]) * scale[None, :]).astype(jnp.bfloat16)  7 us
    div x1, other arithmetic, on_device(): return summed / samples_total  5.3 us
    another operation x1, other arithmetic, on_device(): partial_value = jnp.stack(results)  4.98 us
  transfers between devices with their start and end apart: 2, of which 2 were waited for; matrix products, arithmetic and copies ran while one was open for 6% of the time, Pallas kernels for 0%

commit v1 on v0

v1 whole, which is shorter than its diff:
```python
import functools

import jax
import jax.numpy as jnp
from jax import lax
from jax.experimental import pallas as pl
from jax.experimental.pallas import tpu as pltpu
from jax.sharding import PartitionSpec as P

BLOCK = 512
REACH = 2
HALF = BLOCK // 2
CHUNK = 256
MESH = pl.DeviceIdType.MESH
F32 = jnp.float32
BF16 = jnp.bfloat16
PIECES = ((0, 256), (256, 256), (512, 256), (768, 256))


def tiles_of(start):
    block = 3 + start // BLOCK
    return [(local, block - local) for local in range(3) if block - local <= REACH]


def ld_kernel(
    runs, samples_total, x_hbm, out_ref, xv, sv, svt, halo, hs, part, got, sums, sums_peer,
    stats, halo_stats, load_sem, sum_sems, stat_sems, halo_send, halo_recv, tile_send, tile_recv,
):
    r = lax.axis_index("region")
    s = lax.axis_index("snp")
    c = lax.axis_index("sample")
    peer = (r, s, 1 - c)
    left = (r, s - 1, c)
    right = (r, s + 1, c)
    rows, width = xv.shape
    has_left = s > 0
    has_right = s < runs - 1

    barrier = pltpu.get_barrier_semaphore()
    load = pltpu.make_async_copy(x_hbm, xv, load_sem)
    load.start()
    pl.semaphore_signal(barrier, inc=1, device_id=peer, device_id_type=MESH)

    @pl.when(has_right)
    def _():
        pl.semaphore_signal(barrier, inc=1, device_id=right, device_id_type=MESH)

    pl.semaphore_wait(barrier, jnp.where(has_left, 2, 1))

    def halo_copy(k):
        start, size = PIECES[k]
        cols = pl.ds(start, size)
        return pltpu.make_async_remote_copy(
            x_hbm.at[:, cols], halo.at[:, cols], halo_send.at[k], halo_recv.at[k],
            device_id=left, device_id_type=MESH,
        )

    @pl.when(has_left)
    def _():
        for k in range(2):
            halo_copy(k).start()

    load.wait()

    def add_rows(i, carry):
        a, b = carry
        v = xv[pl.ds(pl.multiple_of(i * 16, 16), 16), :].astype(F32)
        q = v * v
        return a + (v[:8] + v[8:]), b + (q[:8] + q[8:])

    zero = jnp.zeros((8, width), F32)
    a, b = lax.fori_loop(0, rows // 16, add_rows, (zero, zero))
    sums[0:1, :] = jnp.sum(a, axis=0, keepdims=True)
    sums[1:2, :] = jnp.sum(b, axis=0, keepdims=True)
    sums[2:8, :] = jnp.zeros((6, width), F32)
    swap = pltpu.make_async_remote_copy(
        sums, sums_peer, sum_sems.at[0], sum_sems.at[1], device_id=peer, device_id_type=MESH
    )
    swap.start()
    swap.wait()
    both = sums[...] + sums_peer[...]
    mean = both[0:1] / samples_total
    variance = both[1:2] / samples_total - mean * mean
    scale = lax.rsqrt(variance + 1e-05)
    stats[0:1, :] = mean
    stats[1:2, :] = scale
    stats[2:8, :] = jnp.zeros((6, width), F32)
    stat_copy = pltpu.make_async_remote_copy(
        stats.at[:, pl.ds(0, REACH * BLOCK)], halo_stats, stat_sems.at[0], stat_sems.at[1],
        device_id=left, device_id_type=MESH,
    )

    @pl.when(has_left)
    def _():
        stat_copy.start()

    def standardize(i, _):
        at = pl.ds(pl.multiple_of(i * 256, 256), 256)
        for col in range(0, width, BLOCK):
            cols = pl.ds(col, BLOCK)
            v = xv[at, cols].astype(F32)
            w = ((v - stats[0:1, cols]) * stats[1:2, cols]).astype(BF16)
            sv[at, cols] = w
            svt[cols, at] = w.T
        return 0

    lax.fori_loop(0, rows // 256, standardize, 0)

    def tile_copy(n, tile, cols):
        at = pl.ds(pl.multiple_of(tile * BLOCK + (1 - c) * HALF, HALF), HALF)
        return pltpu.make_async_remote_copy(
            part.at[at, cols], got.at[pl.ds(tile * HALF, HALF), cols],
            tile_send.at[n], tile_recv.at[n], device_id=peer, device_id_type=MESH,
        )

    def finish(n, tile, cols):
        copy = tile_copy(n, tile, cols)
        copy.wait()
        own = pl.ds(pl.multiple_of(tile * BLOCK + c * HALF, HALF), HALF)
        at = pl.ds(tile * HALF, HALF)
        out_ref[at, cols] = (part[own, cols] + got[at, cols]) * (1.0 / samples_total)

    whole = pl.ds(0, BLOCK)
    local = [(b0, off) for b0 in range(3) for off in range(3 - b0)]
    for n, (b0, off) in enumerate(local):
        tile = b0 * 3 + off
        part[tile * BLOCK : (tile + 1) * BLOCK, :] = jnp.dot(
            svt[b0 * BLOCK : (b0 + 1) * BLOCK, :],
            sv[:, (b0 + off) * BLOCK : (b0 + off + 1) * BLOCK],
            preferred_element_type=F32,
        )
        tile_copy(n, tile, whole).start()
    for n, (b0, off) in enumerate(local):
        finish(n, b0 * 3 + off, whole)

    @pl.when(has_left)
    def _():
        stat_copy.wait_send()

    @pl.when(has_right)
    def _():
        stat_copy.wait_recv()

    n = len(local)
    pending = []
    for k, (start, size) in enumerate(PIECES):

        @pl.when(has_left)
        def _():
            halo_copy(k).wait_send()
            if k + 2 < len(PIECES):
                halo_copy(k + 2).start()

        here = tiles_of(start)
        at_col = start % BLOCK
        cols = pl.ds(at_col, size)

        @pl.when(has_right)
        def _():
            halo_copy(k).wait_recv()

            def standardize_halo(i, _):
                at = pl.ds(pl.multiple_of(i * 256, 256), 256)
                hc = pl.ds(start, size)
                v = halo[at, hc].astype(F32)
                hs[at, 0:size] = ((v - halo_stats[0:1, hc]) * halo_stats[1:2, hc]).astype(BF16)
                return 0

            lax.fori_loop(0, rows // 256, standardize_halo, 0)
            for j, (b0, off) in enumerate(here):
                tile = b0 * 3 + off
                part[tile * BLOCK : (tile + 1) * BLOCK, at_col : at_col + size] = jnp.dot(
                    svt[b0 * BLOCK : (b0 + 1) * BLOCK, :], hs[:, 0:size],
                    preferred_element_type=F32,
                )
                tile_copy(n + j, tile, cols).start()
            for j, (b0, off) in enumerate(here):
                finish(n + j, b0 * 3 + off, cols)

        n += len(here)

    @pl.when(jnp.logical_not(has_right))
    def _():
        for tile in (5, 7, 8):
            out_ref[tile * HALF : (tile + 1) * HALF, :] = jnp.zeros((HALF, BLOCK), F32)


def pick_kernel(partners_ref, tiles_ref, out_ref):
    b = pl.program_id(0)
    base = partners_ref[b, 0]
    out_ref[0, 0] = tiles_ref[0, 0]
    p1 = partners_ref[b, 1]
    p2 = partners_ref[b, 2]
    one = tiles_ref[0, 1]
    two = tiles_ref[0, 2]
    zero = jnp.zeros_like(one)
    out_ref[0, 1] = jnp.where(p1 < 0, zero, jnp.where(p1 == base + 1, one, two))
    out_ref[0, 2] = jnp.where(p2 < 0, zero, two)


def on_device(dosage, partners):
    rows, width = dosage.shape
    samples_total = rows * lax.axis_size("sample")
    blocks = partners.shape[0]
    tiles = blocks * 3
    n_cross = sum(len(tiles_of(start)) for start, _ in PIECES)
    n_copies = 6 + n_cross
    dma = pltpu.SemaphoreType.DMA
    sums = pl.pallas_call(
        functools.partial(ld_kernel, lax.axis_size("snp"), samples_total),
        out_shape=jax.ShapeDtypeStruct((tiles * HALF, BLOCK), F32),
        in_specs=[pl.BlockSpec(memory_space=pl.ANY)],
        out_specs=pl.BlockSpec(memory_space=pltpu.VMEM),
        scratch_shapes=[
            pltpu.VMEM((rows, width), BF16),
            pltpu.VMEM((rows, width), BF16),
            pltpu.VMEM((width, rows), BF16),
            pltpu.VMEM((rows, REACH * BLOCK), BF16),
            pltpu.VMEM((rows, CHUNK), BF16),
            pltpu.VMEM((tiles * BLOCK, BLOCK), F32),
            pltpu.VMEM((tiles * HALF, BLOCK), F32),
            pltpu.VMEM((8, width), F32),
            pltpu.VMEM((8, width), F32),
            pltpu.VMEM((8, width), F32),
            pltpu.VMEM((8, REACH * BLOCK), F32),
            dma,
            dma((2,)),
            dma((2,)),
            dma((len(PIECES),)),
            dma((len(PIECES),)),
            dma((n_copies,)),
            dma((n_copies,)),
        ],
        compiler_params=pltpu.CompilerParams(
            collective_id=0, has_side_effects=True, vmem_limit_bytes=52 * 2**20
        ),
    )(dosage)
    return pl.pallas_call(
        pick_kernel,
        grid=(blocks,),
        out_shape=jax.ShapeDtypeStruct((blocks, 3, HALF, BLOCK), F32),
        in_specs=[
            pl.BlockSpec(memory_space=pltpu.SMEM),
            pl.BlockSpec((1, 3, HALF, BLOCK), lambda b: (b, 0, 0, 0)),
        ],
        out_specs=pl.BlockSpec((1, 3, HALF, BLOCK), lambda b: (b, 0, 0, 0)),
        compiler_params=pltpu.CompilerParams(vmem_limit_bytes=24 * 2**20),
    )(partners, sums.reshape(blocks, 3, HALF, BLOCK))


def solution(mesh):
    in_specs = (P("sample", ("region", "snp")), P(("region", "snp"), None))
    out_specs = P(("region", "snp"), None, "sample", None)
    return jax.shard_map(
        on_device, mesh=mesh, in_specs=in_specs, out_specs=out_specs, check_vma=False
    )
```

time: 229 us -> 107 us (0.47)
  waiting for transfers between devices: 144 us -> 0 us
  Pallas kernels: 0 us -> 105 us
  other arithmetic: 30.9 us -> 0 us
  matrix products: 21.6 us -> 0 us
  between operations: 13.5 us -> 0.03 us
  local copies, waits for them, and re-layouts: 12.7 us -> 2.33 us
  blocking collectives: 3.57 us -> 0 us
    ppermute x1 -> x0, waiting for transfers between devices: 125 us -> none  [shifted(): return lax.ppermute(block, axis, route)]
    pallas_call x0 -> x2, Pallas kernels: none -> 105 us  [the longest x1 102 us: on_device(): pl.pallas_call(functools.partial(ld_kernel, lax.axis_size('snp'), samples...]
    dot_general x3 -> x0, matrix products: 21.6 us -> none  [panel_product(): lax.dot_general(own, panel, (((0,), (0,)), ((), ())), preferred_element_t...]
    reduce_scatter x1 -> x0, waiting for transfers between devices: 19.3 us -> none  [on_device(): lax.psum_scatter(partial_value, 'sample', scatter_dimension=2, tiled=True)]
    reduce_sum x4 -> x0, other arithmetic: 11.6 us -> none  [the longest x3 7.11 us: on_device(): results.append(jnp.sum(picked, axis=1))]
    transpose x3 -> x0, local copies, waits for them, and re-layouts: 9.52 us -> none  [on_device(): panel_product(own, panel).reshape(width, REACH + 1, width)]
    convert_element_type x1 -> x0, other arithmetic: 7 us -> none  [on_device(): standard = ((values - mean[None, :]) * scale[None, :]).astype(jnp.bfloat16)]
    div x2 -> x0, other arithmetic: 5.31 us -> none  [the longest x1 5.3 us: on_device(): return summed / samples_total]
  transfers between devices with their start and end apart: 2 -> 0, of which waited for: 2 -> 0; matrix products, arithmetic and copies ran while one was open for 6% -> 0% of each run, Pallas kernels for 0% -> 0%
where the time goes in v1:
time: 107 us
  Pallas kernels  105 us (98%)
  local copies, waits for them, and re-layouts  2.33 us (2%)
    pallas_call x1, Pallas kernels, on_device(): pl.pallas_call(functools.partial(ld_kernel, lax.axis_size('snp'), samples...  102 us
    pallas_call x1, Pallas kernels, on_device(): pl.pallas_call(pick_kernel, grid=(blocks,), out_shape=jax.ShapeDtypeStruc...  3.08 us
    unnamed x4, local copies, waits for them, and re-layouts  2.33 us

profile of v1, /device:TPU:0, one launch (start us, length us, event | category | flops | bytes accessed | tf_op | source)
XLA Modules:
  0.0 107.2 jit_solution(2730907227465984931)
XLA Ops:
  0.0 0.0 copy-start.1
  0.0 101.7 %shard_map.28 = f32[2304,512]{1,0:T(8,128)} custom-call(bf16[2048,1536]{1,0:T(8,128)(2,1)} %x_hbm.1), custom_call_target="tpu_custom_call" | custom-call | tf_op jit(solution)/shard_map/pallas_call | solution.py:209
  101.7 0.0 copy-done.1
  101.7 0.0 copy-start
  101.8 2.3 %copy-done = f32[2304,512]{1,0:T(8,128)S(1)} copy-done((f32[2304,512]{1,0:T(8,128)S(1)}, f32[2304,512]{1,0:T(8,128)}, u32[]{:S(2)}) %copy-start) | copy-done | bytes 4718616
  104.1 3.1 %shard_map.29 = f32[3,3,256,512]{3,2,1,0:T(8,128)} custom-call(s32[3,3]{1,0:T(4,128)S(1)} %copy-done.1, f32[3,3,256,512]{3,2,1,0:T(8,128)S(1)} %bitcast.1), custom_call_target="tpu_custom_call" | custom-call | tf_op jit(solution)/shard_map/pallas_call | solution.py:238
Async XLA Ops:
  0.0 101.7 %copy-start.1 = (s32[3,3]{1,0:T(4,128)S(1)}, s32[3,3]{1,0:T(4,128)}, u32[]{:S(2)}) copy-start(s32[3,3]{1,0:T(4,128)} %partners_ref.1) | copy-start | bytes 112
  101.7 2.3 %copy-start = (f32[2304,512]{1,0:T(8,128)S(1)}, f32[2304,512]{1,0:T(8,128)}, u32[]{:S(2)}) copy-start(f32[2304,512]{1,0:T(8,128)} %shard_map.28) | copy-start | bytes 14155780

commit v2 on v1

--- a/solution.py
+++ b/solution.py
@@ -14,7 +14,7 @@
 MESH = pl.DeviceIdType.MESH
 F32 = jnp.float32
 BF16 = jnp.bfloat16
-PIECES = ((0, 256), (256, 256), (512, 256), (768, 256))
+PIECES = ((0, 256), (256, 256), (512, 256), (768, 128), (896, 128))
 
 
 def tiles_of(start):
@@ -167,13 +167,16 @@
                 return 0
 
             lax.fori_loop(0, rows // 256, standardize_halo, 0)
-            for j, (b0, off) in enumerate(here):
-                tile = b0 * 3 + off
-                part[tile * BLOCK : (tile + 1) * BLOCK, at_col : at_col + size] = jnp.dot(
-                    svt[b0 * BLOCK : (b0 + 1) * BLOCK, :], hs[:, 0:size],
-                    preferred_element_type=F32,
-                )
-                tile_copy(n + j, tile, cols).start()
+            for half in (1 - c, c):
+                for j, (b0, off) in enumerate(here):
+                    tile = b0 * 3 + off
+                    mine = pl.ds(pl.multiple_of(b0 * BLOCK + half * HALF, HALF), HALF)
+                    at = pl.ds(pl.multiple_of(tile * BLOCK + half * HALF, HALF), HALF)
+                    part[at, cols] = jnp.dot(
+                        svt[mine, :], hs[:, 0:size], preferred_element_type=F32
+                    )
+                    if half is not c:
+                        tile_copy(n + j, tile, cols).start()
             for j, (b0, off) in enumerate(here):
                 finish(n + j, b0 * 3 + off, cols)
 
@@ -185,17 +188,45 @@
             out_ref[tile * HALF : (tile + 1) * HALF, :] = jnp.zeros((HALF, BLOCK), F32)
 
 
-def pick_kernel(partners_ref, tiles_ref, out_ref):
-    b = pl.program_id(0)
-    base = partners_ref[b, 0]
-    out_ref[0, 0] = tiles_ref[0, 0]
-    p1 = partners_ref[b, 1]
-    p2 = partners_ref[b, 2]
-    one = tiles_ref[0, 1]
-    two = tiles_ref[0, 2]
-    zero = jnp.zeros_like(one)
-    out_ref[0, 1] = jnp.where(p1 < 0, zero, jnp.where(p1 == base + 1, one, two))
-    out_ref[0, 2] = jnp.where(p2 < 0, zero, two)
+def pick_kernel(partners_ref, tiles_ref, out_ref, zeros, sems):
+    blocks = out_ref.shape[0]
+    zeros[...] = jnp.zeros_like(zeros)
+
+    def copy(b, slot, src):
+        return pltpu.make_async_copy(src, out_ref.at[b, slot], sems.at[b * 3 + slot])
+
+    def tile(b, off):
+        return tiles_ref.at[pl.ds((b * 3 + off) * HALF, HALF)]
+
+    for b in range(blocks):
+        base = partners_ref[b, 0]
+        p1 = partners_ref[b, 1]
+        p2 = partners_ref[b, 2]
+        copy(b, 0, tile(b, 0)).start()
+
+        @pl.when(p1 == base + 1)
+        def _():
+            copy(b, 1, tile(b, 1)).start()
+
+        @pl.when(p1 == base + 2)
+        def _():
+            copy(b, 1, tile(b, 2)).start()
+
+        @pl.when(p1 < 0)
+        def _():
+            copy(b, 1, zeros).start()
+
+        @pl.when(p2 >= 0)
+        def _():
+            copy(b, 2, tile(b, 2)).start()
+
+        @pl.when(p2 < 0)
+        def _():
+            copy(b, 2, zeros).start()
+
+    for b in range(blocks):
+        for slot in range(3):
+            copy(b, slot, zeros).wait()
 
 
 def on_device(dosage, partners):
@@ -208,7 +239,7 @@
     dma = pltpu.SemaphoreType.DMA
     sums = pl.pallas_call(
         functools.partial(ld_kernel, lax.axis_size("snp"), samples_total),
-        out_shape=jax.ShapeDtypeStruct((tiles * HALF, BLOCK), F32),
+        out_shape=pltpu.VMEM((tiles * HALF, BLOCK), F32),
         in_specs=[pl.BlockSpec(memory_space=pl.ANY)],
         out_specs=pl.BlockSpec(memory_space=pltpu.VMEM),
         scratch_shapes=[
@@ -237,15 +268,15 @@
     )(dosage)
     return pl.pallas_call(
         pick_kernel,
-        grid=(blocks,),
         out_shape=jax.ShapeDtypeStruct((blocks, 3, HALF, BLOCK), F32),
         in_specs=[
             pl.BlockSpec(memory_space=pltpu.SMEM),
-            pl.BlockSpec((1, 3, HALF, BLOCK), lambda b: (b, 0, 0, 0)),
+            pl.BlockSpec(memory_space=pltpu.VMEM),
         ],
-        out_specs=pl.BlockSpec((1, 3, HALF, BLOCK), lambda b: (b, 0, 0, 0)),
-        compiler_params=pltpu.CompilerParams(vmem_limit_bytes=24 * 2**20),
-    )(partners, sums.reshape(blocks, 3, HALF, BLOCK))
+        out_specs=pl.BlockSpec(memory_space=pl.ANY),
+        scratch_shapes=[pltpu.VMEM((HALF, BLOCK), F32), dma((tiles,))],
+        compiler_params=pltpu.CompilerParams(vmem_limit_bytes=16 * 2**20),
+    )(partners, sums)
 
 
 def solution(mesh):

time: 107 us -> 102 us (0.953)
  Pallas kernels: 105 us -> 102 us
  local copies, waits for them, and re-layouts: 2.33 us -> 0.01 us
    pallas_call x1, Pallas kernels: 102 us -> 99.1 us  [on_device(): pl.pallas_call(functools.partial(ld_kernel, lax.axis_size('snp'), samples...]
    unnamed x4 -> x2, local copies, waits for them, and re-layouts: 2.33 us -> 0.01 us
where the time goes in v2:
time: 102 us
  Pallas kernels  102 us (100%)
    pallas_call x1, Pallas kernels, on_device(): pl.pallas_call(functools.partial(ld_kernel, lax.axis_size('snp'), samples...  99.1 us
    pallas_call x1, Pallas kernels, on_device(): pl.pallas_call(pick_kernel, out_shape=jax.ShapeDtypeStruct((blocks, 3, HA...  2.82 us

profile of v2, /device:TPU:0, one launch (start us, length us, event | category | flops | bytes accessed | tf_op | source)
XLA Modules:
  0.0 101.9 jit_solution(1604655215284888754)
XLA Ops:
  0.0 0.0 copy-start
  0.0 99.1 %shard_map.28.tiles_ref = f32[2304,512]{1,0:T(8,128)S(1)} custom-call(bf16[2048,1536]{1,0:T(8,128)(2,1)} %x_hbm.1), custom_call_target="tpu_custom_call" | custom-call | tf_op jit(solution)/shard_map/pallas_call | solution.py:240
  99.1 0.0 copy-done
  99.1 2.8 %shard_map.29 = f32[3,3,256,512]{3,2,1,0:T(8,128)} custom-call(s32[3,3]{1,0:T(4,128)S(1)} %copy-done, f32[2304,512]{1,0:T(8,128)S(1)} %shard_map.28.tiles_ref), custom_call_target="tpu_custom_call" | custom-call | tf_op jit(solution)/shard_map/pallas_call | solution.py:269
Async XLA Ops:
  0.0 99.1 %copy-start = (s32[3,3]{1,0:T(4,128)S(1)}, s32[3,3]{1,0:T(4,128)}, u32[]{:S(2)}) copy-start(s32[3,3]{1,0:T(4,128)} %partners_ref.1) | copy-start | bytes 112

commit v3 on v2

--- a/solution.py
+++ b/solution.py
@@ -14,6 +14,7 @@
 MESH = pl.DeviceIdType.MESH
 F32 = jnp.float32
 BF16 = jnp.bfloat16
+AHEAD = 3
 PIECES = ((0, 256), (256, 256), (512, 256), (768, 128), (896, 128))
 
 
@@ -57,7 +58,7 @@
 
     @pl.when(has_left)
     def _():
-        for k in range(2):
+        for k in range(AHEAD):
             halo_copy(k).start()
 
     load.wait()
@@ -148,8 +149,8 @@
         @pl.when(has_left)
         def _():
             halo_copy(k).wait_send()
-            if k + 2 < len(PIECES):
-                halo_copy(k + 2).start()
+            if k + AHEAD < len(PIECES):
+                halo_copy(k + AHEAD).start()
 
         here = tiles_of(start)
         at_col = start % BLOCK

time: 102 us -> 102 us (level)
  no operation moved by 1% of the time
where the time goes in v3:
time: 102 us
  Pallas kernels  102 us (100%)
    pallas_call x1, Pallas kernels, on_device(): pl.pallas_call(functools.partial(ld_kernel, lax.axis_size('snp'), samples...  99.1 us
    pallas_call x1, Pallas kernels, on_device(): pl.pallas_call(pick_kernel, out_shape=jax.ShapeDtypeStruct((blocks, 3, HA...  2.82 us

profile of v3, /device:TPU:0, one launch (start us, length us, event | category | flops | bytes accessed | tf_op | source)
XLA Modules:
  0.0 101.9 jit_solution(11729342651355262438)
XLA Ops:
  0.0 0.0 copy-start
  0.0 99.1 %shard_map.28.tiles_ref = f32[2304,512]{1,0:T(8,128)S(1)} custom-call(bf16[2048,1536]{1,0:T(8,128)(2,1)} %x_hbm.1), custom_call_target="tpu_custom_call" | custom-call | tf_op jit(solution)/shard_map/pallas_call | solution.py:241
  99.1 0.0 copy-done
  99.1 2.8 %shard_map.29 = f32[3,3,256,512]{3,2,1,0:T(8,128)} custom-call(s32[3,3]{1,0:T(4,128)S(1)} %copy-done, f32[2304,512]{1,0:T(8,128)S(1)} %shard_map.28.tiles_ref), custom_call_target="tpu_custom_call" | custom-call | tf_op jit(solution)/shard_map/pallas_call | solution.py:270
Async XLA Ops:
  0.0 99.1 %copy-start = (s32[3,3]{1,0:T(4,128)S(1)}, s32[3,3]{1,0:T(4,128)}, u32[]{:S(2)}) copy-start(s32[3,3]{1,0:T(4,128)} %partners_ref.1) | copy-start | bytes 112

commit v4 on v2

--- a/solution.py
+++ b/solution.py
@@ -14,7 +14,14 @@
 MESH = pl.DeviceIdType.MESH
 F32 = jnp.float32
 BF16 = jnp.bfloat16
-PIECES = ((0, 256), (256, 256), (512, 256), (768, 128), (896, 128))
+PIECES = (
+    (0, 256, 0, 8),
+    (256, 256, 0, 8),
+    (512, 256, 0, 8),
+    (768, 128, 0, 8),
+    (896, 128, 0, 6),
+    (896, 128, 6, 8),
+)
 
 
 def tiles_of(start):
@@ -48,10 +55,11 @@
     pl.semaphore_wait(barrier, jnp.where(has_left, 2, 1))
 
     def halo_copy(k):
-        start, size = PIECES[k]
+        start, size, first, last = PIECES[k]
         cols = pl.ds(start, size)
+        at = pl.ds(first * rows // 8, (last - first) * rows // 8)
         return pltpu.make_async_remote_copy(
-            x_hbm.at[:, cols], halo.at[:, cols], halo_send.at[k], halo_recv.at[k],
+            x_hbm.at[at, cols], halo.at[at, cols], halo_send.at[k], halo_recv.at[k],
             device_id=left, device_id_type=MESH,
         )
 
@@ -143,7 +151,7 @@
 
     n = len(local)
     pending = []
-    for k, (start, size) in enumerate(PIECES):
+    for k, (start, size, first, last) in enumerate(PIECES):
 
         @pl.when(has_left)
         def _():
@@ -166,21 +174,25 @@
                 hs[at, 0:size] = ((v - halo_stats[0:1, hc]) * halo_stats[1:2, hc]).astype(BF16)
                 return 0
 
-            lax.fori_loop(0, rows // 256, standardize_halo, 0)
+            row0, row1 = first * rows // 8, last * rows // 8
+            lax.fori_loop(row0 // 256, row1 // 256, standardize_halo, 0)
             for half in (1 - c, c):
                 for j, (b0, off) in enumerate(here):
                     tile = b0 * 3 + off
                     mine = pl.ds(pl.multiple_of(b0 * BLOCK + half * HALF, HALF), HALF)
                     at = pl.ds(pl.multiple_of(tile * BLOCK + half * HALF, HALF), HALF)
-                    part[at, cols] = jnp.dot(
-                        svt[mine, :], hs[:, 0:size], preferred_element_type=F32
+                    term = jnp.dot(
+                        svt[mine, row0:row1], hs[row0:row1, 0:size], preferred_element_type=F32
                     )
-                    if half is not c:
+                    part[at, cols] = term if first == 0 else part[at, cols] + term
+                    if half is not c and last == 8:
                         tile_copy(n + j, tile, cols).start()
-            for j, (b0, off) in enumerate(here):
-                finish(n + j, b0 * 3 + off, cols)
-
-        n += len(here)
+            if last == 8:
+                for j, (b0, off) in enumerate(here):
+                    finish(n + j, b0 * 3 + off, cols)
+
+        if last == 8:
+            n += len(here)
 
     @pl.when(jnp.logical_not(has_right))
     def _():
@@ -190,19 +202,19 @@
 
 def pick_kernel(partners_ref, tiles_ref, out_ref, zeros, sems):
     blocks = out_ref.shape[0]
-    zeros[...] = jnp.zeros_like(zeros)
-
     def copy(b, slot, src):
         return pltpu.make_async_copy(src, out_ref.at[b, slot], sems.at[b * 3 + slot])
 
     def tile(b, off):
         return tiles_ref.at[pl.ds((b * 3 + off) * HALF, HALF)]
 
+    for b in range(blocks):
+        copy(b, 0, tile(b, 0)).start()
+    zeros[...] = jnp.zeros_like(zeros)
     for b in range(blocks):
         base = partners_ref[b, 0]
         p1 = partners_ref[b, 1]
         p2 = partners_ref[b, 2]
-        copy(b, 0, tile(b, 0)).start()
 
         @pl.when(p1 == base + 1)
         def _():
@@ -234,7 +246,7 @@
     samples_total = rows * lax.axis_size("sample")
     blocks = partners.shape[0]
     tiles = blocks * 3
-    n_cross = sum(len(tiles_of(start)) for start, _ in PIECES)
+    n_cross = sum(len(tiles_of(start)) for start, _, _, last in PIECES if last == 8)
     n_copies = 6 + n_cross
     dma = pltpu.SemaphoreType.DMA
     sums = pl.pallas_call(

time: 102 us -> 102 us (level)
  no operation moved by 1% of the time
where the time goes in v4:
time: 102 us
  Pallas kernels  102 us (100%)
    pallas_call x1, Pallas kernels, on_device(): pl.pallas_call(functools.partial(ld_kernel, lax.axis_size('snp'), samples...  98.8 us
    pallas_call x1, Pallas kernels, on_device(): pl.pallas_call(pick_kernel, out_shape=jax.ShapeDtypeStruct((blocks, 3, HA...  2.82 us

profile of v4, /device:TPU:0, one launch (start us, length us, event | category | flops | bytes accessed | tf_op | source)
XLA Modules:
  0.0 101.6 jit_solution(15686635506071435271)
XLA Ops:
  0.0 0.0 copy-start
  0.0 98.8 %shard_map.28.tiles_ref = f32[2304,512]{1,0:T(8,128)S(1)} custom-call(bf16[2048,1536]{1,0:T(8,128)(2,1)} %x_hbm.1), custom_call_target="tpu_custom_call" | custom-call | tf_op jit(solution)/shard_map/pallas_call | solution.py:252
  98.8 0.0 copy-done
  98.8 2.8 %shard_map.29 = f32[3,3,256,512]{3,2,1,0:T(8,128)} custom-call(s32[3,3]{1,0:T(4,128)S(1)} %copy-done, f32[2304,512]{1,0:T(8,128)S(1)} %shard_map.28.tiles_ref), custom_call_target="tpu_custom_call" | custom-call | tf_op jit(solution)/shard_map/pallas_call | solution.py:281
Async XLA Ops:
  0.0 98.8 %copy-start = (s32[3,3]{1,0:T(4,128)S(1)}, s32[3,3]{1,0:T(4,128)}, u32[]{:S(2)}) copy-start(s32[3,3]{1,0:T(4,128)} %partners_ref.1) | copy-start | bytes 112

commit v5 on v4

--- a/solution.py
+++ b/solution.py
@@ -200,8 +200,10 @@
             out_ref[tile * HALF : (tile + 1) * HALF, :] = jnp.zeros((HALF, BLOCK), F32)
 
 
-def pick_kernel(partners_ref, tiles_ref, out_ref, zeros, sems):
+def pick_kernel(partners_any, tiles_ref, out_ref, partners_ref, zeros, fetch_sem, sems):
     blocks = out_ref.shape[0]
+    fetch = pltpu.make_async_copy(partners_any, partners_ref, fetch_sem)
+    fetch.start()
     def copy(b, slot, src):
         return pltpu.make_async_copy(src, out_ref.at[b, slot], sems.at[b * 3 + slot])
 
@@ -211,6 +213,7 @@
     for b in range(blocks):
         copy(b, 0, tile(b, 0)).start()
     zeros[...] = jnp.zeros_like(zeros)
+    fetch.wait()
     for b in range(blocks):
         base = partners_ref[b, 0]
         p1 = partners_ref[b, 1]
@@ -282,11 +285,16 @@
         pick_kernel,
         out_shape=jax.ShapeDtypeStruct((blocks, 3, HALF, BLOCK), F32),
         in_specs=[
-            pl.BlockSpec(memory_space=pltpu.SMEM),
+            pl.BlockSpec(memory_space=pl.ANY),
             pl.BlockSpec(memory_space=pltpu.VMEM),
         ],
         out_specs=pl.BlockSpec(memory_space=pl.ANY),
-        scratch_shapes=[pltpu.VMEM((HALF, BLOCK), F32), dma((tiles,))],
+        scratch_shapes=[
+            pltpu.SMEM(partners.shape, jnp.int32),
+            pltpu.VMEM((HALF, BLOCK), F32),
+            dma,
+            dma((tiles,)),
+        ],
         compiler_params=pltpu.CompilerParams(vmem_limit_bytes=16 * 2**20),
     )(partners, sums)
 

time: 102 us -> 101 us (level)
  no operation moved by 1% of the time
where the time goes in v5:
time: 101 us
  Pallas kernels  101 us (100%)
    pallas_call x1, Pallas kernels, on_device(): pl.pallas_call(functools.partial(ld_kernel, lax.axis_size('snp'), samples...  98.8 us
    pallas_call x1, Pallas kernels, on_device(): pl.pallas_call(pick_kernel, out_shape=jax.ShapeDtypeStruct((blocks, 3, HA...  2.31 us

profile of v5, /device:TPU:0, one launch (start us, length us, event | category | flops | bytes accessed | tf_op | source)
XLA Modules:
  0.0 101.1 jit_solution(7898463490562435696)
XLA Ops:
  0.0 0.0 copy-start
  0.0 98.8 %shard_map.28.tiles_ref = f32[2304,512]{1,0:T(8,128)S(1)} custom-call(bf16[2048,1536]{1,0:T(8,128)(2,1)} %x_hbm.1), custom_call_target="tpu_custom_call" | custom-call | tf_op jit(solution)/shard_map/pallas_call | solution.py:255
  98.8 0.0 copy-done
  98.8 2.3 %shard_map.29 = f32[3,3,256,512]{3,2,1,0:T(8,128)} custom-call(s32[3,3]{1,0:T(4,128)S(1)} %copy-done, f32[2304,512]{1,0:T(8,128)S(1)} %shard_map.28.tiles_ref), custom_call_target="tpu_custom_call" | custom-call | tf_op jit(solution)/shard_map/pallas_call | solution.py:284
Async XLA Ops:
  0.0 98.8 %copy-start = (s32[3,3]{1,0:T(4,128)S(1)}, s32[3,3]{1,0:T(4,128)}, u32[]{:S(2)}) copy-start(s32[3,3]{1,0:T(4,128)} %partners_any.1) | copy-start | bytes 112
